TPU v7x, 128 devices: a whole 4x4x4 slice. The times are simulated.
128 devices in a mesh: blk: 4 (over y_lo, core), dp: 32 (over z, x, y_hi).
Axes of the slice: x: 4, y: 4 (y_hi: 2, y_lo: 2; y = y_hi * 2 + y_lo), z: 4, core: 2. Of those that a mesh axis runs over, the one named last changes fastest.
Arguments:
- image_features: bfloat16 [16384, 1152], P(('blk', 'dp')), may hold values from -12 to 12
- text_features: bfloat16 [16384, 1152], P(('blk', 'dp')), may hold values from -12 to 12
- image_head: bfloat16 [1152, 1152], replicated, may hold values from -1 to 1
- text_head: bfloat16 [1152, 1152], replicated, may hold values from -1 to 1
- scale: float32 [1], replicated, may hold values from 16 to 64
- offset: float32 [1], replicated, may hold values from -10 to -5
Outputs:
- image_head_grad: float32 [1152, 1152], replicated
- text_head_grad: float32 [1152, 1152], replicated
All inputs are finite; a program needn't handle non-finite values.
Results may differ from a plain program's by a relative error of at most 0.0055.
Values may be sent and summed in bfloat16 or wider, within the bound.
A program may use at most 128 MiB of HBM per device.

v0:
```python
import jax
import jax.numpy as jnp
from jax import lax
from jax.sharding import PartitionSpec as P

EPS = 1e-06


def passed_along(value, axis, by):
    peers = lax.axis_size(axis)
    return lax.ppermute(value, axis, [(i, (i + by) % peers) for i in range(peers)])


def unit_rows(features, head):
    proj = jnp.dot(features, head, preferred_element_type=jnp.float32)
    norm = jnp.sqrt(jnp.sum(proj * proj, axis=-1, keepdims=True) + EPS)
    return (proj / norm, norm)


def pullback(unit, norm, grad):
    return (grad - unit * jnp.sum(unit * grad, axis=-1, keepdims=True)) / norm


def head_term(features, back):
    return jnp.einsum(
        "rd,re->de", features, back.astype(jnp.bfloat16), preferred_element_type=jnp.float32
    )


def pair_coef(image_emb, text_emb, temper, shift_bias, positive):
    logits = (
        temper * jnp.einsum("id,jd->ij", image_emb, text_emb, preferred_element_type=jnp.float32)
        + shift_bias
    )
    return (jax.nn.sigmoid(logits) - positive.astype(jnp.float32)).astype(jnp.bfloat16)


def text_pull(coef, image_emb, temper):
    return temper * jnp.einsum("ij,id->jd", coef, image_emb, preferred_element_type=jnp.float32)


def shards(image_features, text_features, image_head, text_head, scale, offset):
    temper = scale[0]
    shift_bias = offset[0]
    member_id = lax.axis_index("dp")
    rows_dev = image_features.shape[0]
    group_rows = rows_dev * lax.axis_size("dp")
    image_unit, image_norm = unit_rows(image_features, image_head)
    image_emb = image_unit.astype(jnp.bfloat16)
    text_unit, text_norm = unit_rows(text_features, text_head)
    text_emb = text_unit.astype(jnp.bfloat16)
    own_ids = jnp.arange(rows_dev, dtype=jnp.int32)
    arriving = passed_along(text_emb, "blk", 1)
    group_set = lax.all_gather(text_emb, "dp", axis=0, tiled=True)
    visiting = lax.all_gather(arriving, "dp", axis=0, tiled=True)
    set_ids = jnp.arange(group_rows, dtype=jnp.int32)
    diagonal = set_ids[None, :] == member_id * rows_dev + own_ids[:, None]
    nothing = jnp.zeros((rows_dev, group_rows), jnp.bool_)
    coef_own = pair_coef(image_emb, group_set, temper, shift_bias, diagonal)
    coef_prev = pair_coef(image_emb, visiting, temper, shift_bias, nothing)
    image_dir = temper * jnp.dot(
        coef_own, group_set, preferred_element_type=jnp.float32
    ) + temper * jnp.dot(coef_prev, visiting, preferred_element_type=jnp.float32)
    own_share, prev_share = (
        lax.psum_scatter(
            text_pull(coef_own, image_emb, temper).astype(jnp.bfloat16),
            "dp",
            scatter_dimension=0,
            tiled=True,
        ).astype(jnp.float32),
        lax.psum_scatter(
            text_pull(coef_prev, image_emb, temper).astype(jnp.bfloat16),
            "dp",
            scatter_dimension=0,
            tiled=True,
        ).astype(jnp.float32),
    )
    returned = passed_along(prev_share.astype(jnp.bfloat16), "blk", -1).astype(prev_share.dtype)
    text_dir = own_share + returned
    image_term = head_term(image_features, pullback(image_unit, image_norm, image_dir))
    text_term = head_term(text_features, pullback(text_unit, text_norm, text_dir))
    image_grad, text_grad = lax.psum((image_term, text_term), ("blk", "dp"))
    return (image_grad, text_grad)


def solution(mesh):
    in_specs = (P(("blk", "dp"), None), P(("blk", "dp"), None), P(), P(), P(), P())
    out_specs = (P(), P())
    return jax.shard_map(shards, mesh=mesh, in_specs=in_specs, out_specs=out_specs, check_vma=False)
```

profile of v0, /device:TPU:1, one launch (start us, length us, event | category | flops | bytes accessed | tf_op | source)
XLA Modules:
  0.0 923.5 jit_solution(10186979887509862361)
XLA Ops:
  7.2 0.0 copy-start
  7.2 0.0 all-gather.5.cloned.1.call-start
  7.2 1.7 copy-done
  8.9 1.6 multiply_reduce_fusion.2
  10.6 0.0 copy-start.2
  10.6 0.8 copy-done.2
  11.4 0.1 fusion.21
  11.5 0.0 copy-start.6
  11.5 2.8 collective-permute-start
  14.3 3.7 collective-permute-done
  18.0 0.0 copy-start.7
  18.0 0.7 copy-done.7
  18.7 0.0 all-gather.5.cloned.1.call-update
  18.7 0.0 all-gather.3.cloned.1.call-start
  18.7 0.0 copy-done.6
  18.8 0.7 all-gather.3.cloned.1.call-update
  19.4 0.0 reduce-scatter.5.cloned.1.call-start
  20.8 2.6 multiply_reduce_fusion.3
  23.4 0.1 fusion.20
  23.5 108.2 %all-gather.5.cloned.1.call-done = bf16[4096,1152]{1,0:T(8,128)(2,1)} async-done(((bf16[128,1152]{1,0:T(8,128)(2,1)}), bf16[4096,1152]{1,0:T(8,128)(2,1)}) %all-gather.5.cloned.1.call-update) | async-done | bytes 9437200 | tf_op jit(solution)/shard_map/all_gather | solution.py:55
  131.7 6.8 fusion.11
  138.6 5.2 fusion.1
  143.8 0.0 reduce-scatter.5.cloned.1.call-update
  143.8 0.0 reduce-scatter.3.cloned.1.call-start
  143.9 99.4 %all-gather.3.cloned.1.call-done = bf16[4096,1152]{1,0:T(8,128)(2,1)} async-done(((bf16[128,1152]{1,0:T(8,128)(2,1)}), bf16[4096,1152]{1,0:T(8,128)(2,1)}) %all-gather.3.cloned.1.call-update) | async-done | bytes 9437200 | tf_op jit(solution)/shard_map/all_gather | solution.py:54
  243.3 6.9 fusion.14
  250.2 5.1 fusion
  255.3 0.0 reduce-scatter.3.cloned.1.call-update
  255.3 0.0 all-reduce.3.cloned.1.call-start
  255.4 5.4 fusion.22
  260.8 0.0 copy-start.4
  260.8 6.2 multiply_reduce_fusion.1
  267.1 0.0 copy-start.3
  267.1 0.0 copy-start.5
  267.1 221.6 %reduce-scatter.5.cloned.1.call-done = bf16[128,1152]{1,0:T(8,128)(2,1)} async-done(((bf16[4096,1152]{1,0:T(8,128)(2,1)}), bf16[128,1152]{1,0:T(8,128)(2,1)}) %reduce-scatter.5.cloned.1.call-update) | async-done | bytes 294928 | tf_op jit(solution)/shard_map/reduce_scatter | solution.py:71
  488.7 2.1 collective-permute-start.1
  490.8 0.0 copy-done.4
  490.8 4.4 convolution_bitcast_fusion.1
  495.2 238.8 %reduce-scatter.3.cloned.1.call-done = bf16[128,1152]{1,0:T(8,128)(2,1)} async-done(((bf16[4096,1152]{1,0:T(8,128)(2,1)}), bf16[128,1152]{1,0:T(8,128)(2,1)}) %reduce-scatter.3.cloned.1.call-update) | async-done | bytes 294928 | tf_op jit(solution)/shard_map/reduce_scatter | solution.py:65
  734.0 0.0 collective-permute-done.1
  734.0 0.0 copy-done.3
  734.0 1.2 multiply_reduce_fusion
  735.2 0.0 copy-done.5
  735.2 4.3 convolution_bitcast_fusion
  739.5 0.0 all-reduce.3.cloned.1.call-update
  739.5 163.6 %all-reduce.3.cloned.1.call-done = (f32[1152,1152]{0,1:T(8,128)}, f32[1152,1152]{0,1:T(8,128)}) async-done(((f32[1152,1152]{0,1:T(8,128)}, f32[1152,1152]{0,1:T(8,128)}), (f32[1152,1152]{0,1:T(8,128)}, f32[1152,1152]{0,1:T(8,128)})) %all-reduce.3.cloned.1.call-update) | async-done | bytes 10616848 | tf_op jit(solution)/shard_map/psum | solution.py:82
  903.1 6.9 copy.8
  910.0 0.0 copy-start.1
  910.0 7.0 copy.9
  917.0 0.0 copy-done.1
  (3 shorter events, 0.0 us)
Async XLA Ops:
  7.2 1.8 copy-start
  7.2 124.5 %all-gather.5.cloned.1.call-start = ((), (), s32[]{:S(2)}) async-start(), calls=%async_computation.3 | async-start | bytes 9732096 | tf_op jit(solution)/shard_map/all_gather | solution.py:55
  10.6 0.8 copy-start.2
  11.5 7.2 copy-start.6
  11.5 6.4 collective-permute-start
  18.0 0.7 copy-start.7
  18.7 224.6 %all-gather.3.cloned.1.call-start = ((), (), s32[]{:S(2)}) async-start(), calls=%async_computation.2 | async-start | bytes 9732096 | tf_op jit(solution)/shard_map/all_gather | solution.py:54
  19.4 469.2 %reduce-scatter.5.cloned.1.call-start = ((), (), s32[]{:S(2)}) async-start(), calls=%async_computation.5 | async-start | bytes 9732096 | tf_op jit(solution)/shard_map/reduce_scatter | solution.py:71
  143.8 590.2 %reduce-scatter.3.cloned.1.call-start = ((), (), s32[]{:S(2)}) async-start(), calls=%async_computation.4 | async-start | bytes 9732096 | tf_op jit(solution)/shard_map/reduce_scatter | solution.py:65
  255.3 647.8 %all-reduce.3.cloned.1.call-start = ((), (), s32[]{:S(2)}) async-start(), calls=%async_computation.6 | async-start | bytes 21233664 | tf_op jit(solution)/shard_map/psum | solution.py:82
  260.8 230.0 %copy-start.4 = (bf16[128,1152]{1,0:T(8,128)(2,1)S(1)}, bf16[128,1152]{1,0:T(8,128)(2,1)}, u32[]{:S(2)}) copy-start(bf16[128,1152]{1,0:T(8,128)(2,1)} %param.6) | copy-start | bytes 884740
  267.1 466.9 %copy-start.3 = (f32[128,1152]{1,0:T(8,128)S(1)}, f32[128,1152]{1,0:T(8,128)}, u32[]{:S(2)}) copy-start(f32[128,1152]{1,0:T(8,128)} %copy-done.2) | copy-start | bytes 1769476
  267.1 468.1 %copy-start.5 = (bf16[128,1152]{1,0:T(8,128)(2,1)S(1)}, bf16[128,1152]{1,0:T(8,128)(2,1)}, u32[]{:S(2)}) copy-start(bf16[128,1152]{1,0:T(8,128)(2,1)} %param.7) | copy-start | bytes 884740
  488.7 245.3 %collective-permute-start.1 = (bf16[128,1152]{1,0:T(8,128)(2,1)}, bf16[128,1152]{1,0:T(8,128)(2,1)S(1)}, u32[]{:S(2)}, u32[]{:S(2)}) collective-permute-start(bf16[128,1152]{1,0:T(8,128)(2,1)} %reduce-scatter.5.cloned.1.call-done), channel_id=1, source_target_pairs={{0,96},{32,0},{64,32},{96,64},{1,97},{33,1},{65,33},{97,65},{2,98}... | collective-permute-start | bytes 884744 | tf_op jit(solution)/shard_map/ppermute | solution.py:11
  910.0 7.0 copy-start.1
Sparse Core Ops, SparseCore 0:
  18.8 112.8 all-gather.4
  135.3 107.9 all-gather.2
  248.7 239.9 reduce-scatter.4
  493.9 240.0 reduce-scatter.2
  739.6 163.4 all-reduce.2
where the time goes:
time: 924 us
  waiting for transfers between devices  836 us (90%)
  matrix products  48.7 us (5%)
  local copies, waits for them, and re-layouts  17.1 us (2%)
  between operations  15.2 us (2%)
    reduce_scatter x1, waiting for transfers between devices, shards(): lax.psum_scatter(text_pull(coef_own, image_emb, temper).astype(jnp.bfloat...  239 us
    reduce_scatter x1, waiting for transfers between devices, shards(): lax.psum_scatter(text_pull(coef_prev, image_emb, temper).astype(jnp.bfloa...  222 us
    psum x1, waiting for transfers between devices, shards(): image_grad, text_grad = lax.psum((image_term, text_term), ('blk', 'dp'))  164 us
    all_gather x1, waiting for transfers between devices, shards(): visiting = lax.all_gather(arriving, 'dp', axis=0, tiled=True)  108 us
    all_gather x1, waiting for transfers between devices, shards(): group_set = lax.all_gather(text_emb, 'dp', axis=0, tiled=True)  99.4 us
  transfers between devices with their start and end apart: 7, of which 6 were waited for; matrix products, arithmetic and copies ran while one was open for 5% of the time, Pallas kernels for 0%

commit v1 on v0

v1 whole, which is shorter than its diff:
```python
import jax
import jax.numpy as jnp
from jax import lax
from jax.experimental import pallas as pl
from jax.experimental.pallas import tpu as pltpu
from jax.sharding import PartitionSpec as P

EPS = 1e-06
MESH = pl.DeviceIdType.MESH
D = 1152
ROWS = 128
UNIT = 256
UNITS = 5
TILE = 1024
HALF = 64
WIDE = D + 128
SPAN = 240.0


def position():
    blk, dp = lax.axis_index("blk"), lax.axis_index("dp")
    return {"z": dp // 8, "x": (dp // 2) % 4, "hi": dp % 2, "lo": blk // 2, "core": blk % 2}


def device(p):
    return (p["lo"] * 2 + p["core"], p["z"] * 8 + p["x"] * 2 + p["hi"])


def rings_of(p):
    y = p["hi"] * 2 + p["lo"]
    spots = [[(at + d) % 4 for d in range(4)] for at in (p["x"], y, p["z"])]
    places = [
        [{**p, "x": k} for k in spots[0]],
        [{**p, "hi": k // 2, "lo": k % 2} for k in spots[1]],
        [{**p, "z": k} for k in spots[2]],
    ]
    return spots, [[device(q) for q in ring] for ring in places]


def send(src, dst, send_sem, recv_sem, peer):
    return pltpu.make_async_remote_copy(
        src_ref=src, dst_ref=dst, send_sem=send_sem, recv_sem=recv_sem, device_id=peer, device_id_type=MESH
    )


def coded(total):
    top = jnp.max(jnp.abs(total), axis=-1, keepdims=True)
    scale = (jnp.maximum(top, 1e-30) * 1.01).astype(jnp.bfloat16)
    size = jnp.exp2(jnp.abs(total) * (SPAN / scale.astype(jnp.float32)) - SPAN / 2)
    return jnp.where(total < 0, -size, size).astype(jnp.bfloat16), scale


def decoded(rows):
    code = rows[:, :D].astype(jnp.float32)
    size = (jnp.log2(jnp.abs(code)) + SPAN / 2) * (rows[:, D : D + 1].astype(jnp.float32) / SPAN)
    return jnp.where(code < 0, -size, size)


def dot(a, b, over=((1,), (0,))):
    return lax.dot_general(a, b, (over, ((), ())), preferred_element_type=jnp.float32)


def kernel(
    scale, offset, img, txt, img_head, txt_head, out,
    fi, ft, ui, ut, ei, et, ni, nt, coef, back, part, pair, s1, r1, f2, s2, r2, r3, chunk,
    lsem, ts_s, ts_r, is_s, is_r, gi_s, gi_r, gt_s, gt_r,
    osem, p_s, p_r, a_s, a_r, b_s, b_r, c_s, c_r, d_s, d_r, e_s, e_r, m_s, m_r,
):
    p = position()
    x, z, hi, core = p["x"], p["z"], p["hi"], p["core"]
    blk = p["lo"] * 2 + core
    mate = device({**p, "core": 1 - core})
    twin = device({**p, "hi": 1 - hi})
    spots, peers = rings_of(p)

    def of_blk(b, h):
        return device({**p, "lo": b // 2, "core": b % 2, "hi": h})

    nxt = of_blk((blk + 1) % 4, 1)
    before = [of_blk((blk + 3) % 4, h) for h in (0, 1)]
    barrier = pltpu.get_barrier_semaphore()

    def greet(peer):
        pl.semaphore_signal(barrier, inc=1, device_id=peer, device_id_type=MESH)

    for ring in peers:
        for peer in ring[1:]:
            greet(peer)
    greet(mate)

    @pl.when(hi == 1)
    def _():
        greet(before[0])
        greet(before[1])

    wi, wt = part.at[pl.ds(0, D)], part.at[pl.ds(D, D)]
    load_wi = pltpu.make_async_copy(img_head, wi, lsem.at[0])
    load_wt = pltpu.make_async_copy(txt_head, wt, lsem.at[1])
    load_i = pltpu.make_async_copy(img, fi.at[pl.ds((hi * 4 + z) * ROWS, ROWS)], lsem.at[2])
    load_t = pltpu.make_async_copy(txt, ft.at[pl.ds(x * ROWS, ROWS)], lsem.at[3])
    load_i.start()
    load_wi.start()
    load_wt.start()

    @pl.when(hi == 0)
    def _():
        load_t.start()

    pl.semaphore_wait(barrier, 11)


    def piece(ref, h):
        return ref.at[pl.ds(h * HALF, HALF)]

    def rows(ref, s, at, h):
        return ref.at[pl.ds(pl.multiple_of((s * 4 + at) * ROWS + h * HALF, HALF), HALF)]

    def seed_t(k, h):
        return send(piece(txt, h), rows(ft, hi, x, h), ts_s.at[k, h], ts_r.at[hi, h], (nxt, twin)[k])

    def wait_seed_t(s, h):
        send(piece(txt, h), rows(ft, s, x, h), ts_s.at[0, h], ts_r.at[s, h], nxt).wait_recv()

    def seed_i(h):
        return send(piece(img, h), rows(fi, hi, z, h), is_s.at[h], is_r.at[h], twin)

    class Ring:
        def __init__(self, ref, axis, s_sem, r_sem):
            self.ref, self.s_sem, self.r_sem = ref, s_sem, r_sem
            self.spots, self.peers = spots[axis], peers[axis]

        def copy(self, s, kind, src=None):
            h = kind % 2
            at = self.spots[(0, 0, 3, 1)[kind // 2 + (kind == 5)]]
            peer = self.peers[(1, 3, 1, 3)[kind // 2 + (kind == 5)]]
            dst = rows(self.ref, s, at, h)
            return send(dst if src is None else piece(src, h), dst, self.s_sem.at[s, kind], self.r_sem.at[s, kind], peer)

        def start(self, s, h, src=None):
            self.copy(s, h, src).start()
            self.copy(s, 2 + h, src).start()

        def got(self, s, *kinds):
            for kind in kinds:
                self.copy(s, kind).wait_recv()

        def on(self, s):
            self.got(s, 0)
            self.copy(s, 4).start()
            self.got(s, 3)
            self.copy(s, 5).start()

        def sent(self):
            for s in (0, 1):
                for kind in range(6):
                    self.copy(s, kind).wait_send()

    ring_i = Ring(fi, 2, gi_s, gi_r)
    ring_t = Ring(ft, 0, gt_s, gt_r)

    for h in (0, 1):

        @pl.when(hi == 1)
        def _():
            seed_t(0, h).start()
            seed_t(1, h).start()

        @pl.when(hi == 0)
        def _():
            seed_t(0, h).start()
            ring_t.start(0, h, txt)

        ring_i.start(hi, h, img)

    def project(f, w, u, e, n, s, at, first, second):
        spots = [pl.ds(pl.multiple_of((s * 4 + at[k]) * ROWS, ROWS), ROWS) for k in (first, second)]
        proj = dot(jnp.concatenate([f[r] for r in spots], axis=0), w[...])
        inverse = 1.0 / jnp.sqrt(jnp.sum(proj * proj, axis=-1, keepdims=True) + EPS)
        unit = proj * inverse
        low = unit.astype(jnp.bfloat16)
        for k, r in enumerate(spots):
            half = slice(k * ROWS, (k + 1) * ROWS)
            u[r] = unit[half]
            e[r] = low[half]
            n[r] = inverse[half]

    def project_i(s, first, second):
        project(fi, wi, ui, ei, ni, s, spots[2], first, second)

    def project_t(s, first, second):
        project(ft, wt, ut, et, nt, s, spots[0], first, second)

    def texts_arrived(h):
        wait_seed_t(1, h)
        ring_t.start(1, h)

        @pl.when(hi == 1)
        def _():
            wait_seed_t(0, h)
            ring_t.start(0, h)

    texts_arrived(0)
    seed_i(0).start()
    seed_i(1).start()
    ring_i.on(hi)
    texts_arrived(1)
    load_i.wait()
    load_wi.wait()

    @pl.when(hi == 0)
    def _():
        load_t.wait()

    ring_i.got(hi, 1)
    project_i(hi, 0, 3)
    seed_i(0).wait_recv()
    ring_i.start(1 - hi, 0)
    ring_t.on(0)
    ring_i.got(hi, 2, 4, 5)
    project_i(hi, 1, 2)
    ring_t.on(1)
    seed_i(1).wait_recv()
    ring_i.start(1 - hi, 1)
    load_wt.wait()
    ring_t.got(0, 1)
    project_t(0, 0, 3)
    ring_t.got(0, 2, 4, 5)
    project_t(0, 1, 2)
    ring_i.on(1 - hi)
    ring_t.got(1, 1)
    project_t(1, 0, 3)
    ring_i.got(1 - hi, 1)
    project_i(1 - hi, 0, 3)
    ring_t.got(1, 2, 4, 5)
    project_t(1, 1, 2)
    ring_i.got(1 - hi, 2, 4, 5)
    project_i(1 - hi, 1, 2)


    temper = scale[0]
    shift_bias = offset[0]

    def sigmoid_of(a, b):
        logits = temper * dot(a, b, ((1,), (1,))) + shift_bias
        return 1.0 / (1.0 + jnp.exp(-logits))

    for k in range(4):
        r = slice(k * 256, (k + 1) * 256)
        coef[r] = sigmoid_of(ei[r], et[...]).astype(jnp.bfloat16)

    @pl.when(hi == 0)
    def _():
        ids = [lax.broadcasted_iota(jnp.int32, (ROWS, ROWS), k) for k in (0, 1)]
        same = jnp.where(ids[0] == ids[1], 1.0, 0.0)
        for s in (0, 1):
            r = pl.ds(pl.multiple_of((s * 4 + z) * ROWS, ROWS), ROWS)
            c = pl.ds(pl.multiple_of((s * 4 + x) * ROWS, ROWS), ROWS)
            coef[r, c] = (sigmoid_of(ei[r], et[c]) - same).astype(jnp.bfloat16)

    def pull(k, direction, u, n):
        r = slice(k * 256, (k + 1) * 256)
        unit = u[r]
        direction = temper * direction
        along_unit = jnp.sum(unit * direction, axis=-1, keepdims=True)
        back[r] = ((direction - unit * along_unit) * n[r]).astype(jnp.bfloat16)


    def swap(u):
        return send(part.at[pl.ds(u * UNIT, UNIT)], pair.at[u // 2], p_s.at[u // 2], p_r.at[u // 2], mate)

    def give(u):
        @pl.when(core != u % 2)
        def _():
            swap(u).start()

    def by_core(first, second):
        return first + core * (second - first)

    turn_spots = [[by_core(*v) for v in zip(spots[j], spots[(j + 1) % 3])] for j in range(3)]
    turn_peers = [
        [tuple(by_core(*v) for v in zip(*w)) for w in zip(peers[j], peers[(j + 1) % 3])] for j in range(3)
    ]
    core_row = core * UNIT

    def ring_of(l, k):
        return turn_spots[(2 * l + k) % 3], turn_peers[(2 * l + k) % 3]

    def stage1(l, d):
        at, peer = ring_of(l, 0)
        src = s1.at[l, pl.ds(pl.multiple_of(at[d] * 64, 64), 64)]
        return send(src, r1.at[l, d - 1], a_s.at[l, d - 1], a_r.at[l, d - 1], peer[d])

    def stage2(l, d):
        at, peer = ring_of(l, 1)
        src = s2.at[l, pl.ds(pl.multiple_of(at[d] * 16, 16), 16)]
        return send(src, r2.at[l, d - 1], b_s.at[l, d - 1], b_r.at[l, d - 1], peer[d])

    def stage3(l, d):
        at, peer = ring_of(l, 2)
        mine = r3.at[l, at[0]]
        return send(mine, mine, c_s.at[l, d - 1], c_r.at[l, d - 1], peer[d])

    def out_rows(l, first, count):
        return out.at[pl.ds(pl.multiple_of(l * 2 * UNIT + core_row + first, count), count)]

    rows16s = [out_rows(l, ring_of(l, 0)[0][0] * 64 + ring_of(l, 1)[0][0] * 16, 16) for l in range(UNITS)]

    def keep(l):
        return pltpu.make_async_copy(chunk.at[l], rows16s[l], osem.at[l])

    def inner(l, d):
        return send(chunk.at[l], rows16s[l], d_s.at[l, d - 1], d_r.at[l, d - 1], ring_of(l, 1)[1][d])

    def rows64(l, back):
        return out_rows(l, ring_of(l, 0)[0][(4 - back) % 4] * 64, 64)

    def outer(l, d):
        return send(rows64(l, 0), rows64(l, 0), e_s.at[l, d - 1], e_r.at[l, d - 1], ring_of(l, 0)[1][d])

    def over(l, back):
        return send(rows64(l, back), rows64(l, back), m_s.at[l, back], m_r.at[l, back], mate)

    def owned(step):
        def run(l):
            if l < UNITS - 1:
                step(l)
            else:
                pl.when(core == 0)(lambda: step(l))

        return run

    def part_rows(l, k):
        return pl.ds(pl.multiple_of(l * 2 * UNIT + core_row + k * 64, 64), 64)

    @owned
    def begin(l):
        swap(2 * l).wait_recv()

        def block(k, n):
            r = pl.ds(pl.multiple_of(k * 64, 64), 64)
            both = part[part_rows(l, k)].astype(jnp.float32) + pair[l, r].astype(jnp.float32)
            s1[l, r] = both.astype(jnp.bfloat16)
            return n

        lax.fori_loop(0, 4, block, 0)
        for d in (1, 3, 2):
            stage1(l, d).start()

    @owned
    def middle(l):
        for d in (1, 2, 3):
            stage1(l, d).wait_recv()
        k = ring_of(l, 0)[0][0]
        total = part[part_rows(l, k)].astype(jnp.float32)
        total = total + pair[l, pl.ds(pl.multiple_of(k * 64, 64), 64)].astype(jnp.float32)
        for d in range(3):
            total = total + r1[l, d].astype(jnp.float32)
        f2[l] = total
        s2[l] = total.astype(jnp.bfloat16)
        for d in (1, 3, 2):
            stage2(l, d).start()

    @owned
    def last(l):
        for d in (1, 2, 3):
            stage2(l, d).wait_recv()
        total = f2[l, pl.ds(pl.multiple_of(ring_of(l, 1)[0][0] * 16, 16), 16)]
        for d in range(3):
            total = total + r2[l, d].astype(jnp.float32)
        r3[l, ring_of(l, 2)[0][0]] = total
        for d in (1, 3, 2):
            stage3(l, d).start()

    @owned
    def finish(l):
        for d in (1, 2, 3):
            stage3(l, d).wait_recv()
        code, row_scale = coded(((r3[l, 0] + r3[l, 1]) + r3[l, 2]) + r3[l, 3])
        chunk[l, :, :D] = code
        chunk[l, :, D:] = jnp.broadcast_to(row_scale, (16, WIDE - D))
        keep(l).start()
        for d in (1, 3, 2):
            inner(l, d).start()

    @owned
    def around(l):
        keep(l).wait()
        for d in (1, 2, 3):
            inner(l, d).wait_recv()
        for d in (1, 3, 2):
            outer(l, d).start()
        over(l, 0).start()

    @owned
    def across(l):
        for d in (1, 3, 2):
            outer(l, d).wait_recv()
            over(l, d).start()

    @owned
    def drain(l):
        for d in (1, 2, 3):
            for stage in (stage1, stage2, stage3, inner, outer):
                stage(l, d).wait_send()
        for k in range(4):
            over(l, k).wait_send()

    def landed(l, back):
        r = out.at[pl.ds(pl.multiple_of(l * 2 * UNIT + UNIT - core_row + back * 64, 64), 64)]
        return send(r, r, m_s.at[l, back], m_r.at[l, back], mate)

    def arrive(l):
        def go():
            swap(2 * l).wait_send()
            for k in range(4):
                landed(l, k).wait_recv()

        if l < UNITS - 1:
            go()
        else:
            pl.when(core == 1)(go)

    def term(f, row, count, to):
        part[to : to + count] = dot(f[:, row : row + count], back[...], ((0,), (0,))).astype(jnp.bfloat16)

    for k in range(4):
        pull(k, dot(coef[k * 256 : (k + 1) * 256], et[...]), ui, ni)
    for u in range(4):
        term(fi, u * UNIT, UNIT, u * UNIT)
        give(u)
    term(fi, 1024, 128, 1024)

    def pull_text(k):
        pull(k, dot(coef[:, k * 256 : (k + 1) * 256], ei[...], ((0,), (0,))), ut, nt)

    pull_text(0)
    pull_text(1)
    begin(0)
    begin(1)
    pull_text(2)
    pull_text(3)
    term(ft, 0, 128, 1152)
    give(4)
    for u in range(5, 9):
        term(ft, u * UNIT - D, UNIT, u * UNIT)
        give(u)
        if u == 7:
            begin(2)
    begin(3)
    begin(4)
    for step in (middle, last, finish, around, across):
        for l in range(UNITS):
            step(l)


    for h in (0, 1):
        seed_t(0, h).wait_send()
        seed_i(h).wait_send()

        @pl.when(hi == 1)
        def _():
            seed_t(1, h).wait_send()

    ring_i.sent()
    ring_t.sent()
    for l in range(UNITS):
        drain(l)
        arrive(l)


def head_sums(scale, offset, img, txt, img_head, txt_head):
    dma = pltpu.SemaphoreType.DMA
    low, f32 = jnp.bfloat16, jnp.float32
    any_ = pl.BlockSpec(memory_space=pl.ANY)
    smem = pl.BlockSpec(memory_space=pltpu.SMEM)
    return pl.pallas_call(
        kernel,
        out_shape=jax.ShapeDtypeStruct((2 * D, WIDE), low),
        in_specs=[smem] * 2 + [any_] * 4,
        out_specs=any_,
        scratch_shapes=[pltpu.VMEM((TILE, D), low)] * 2
        + [pltpu.VMEM((TILE, D), f32)] * 2
        + [pltpu.VMEM((TILE, D), low)] * 2
        + [pltpu.VMEM((TILE, 1), f32)] * 2
        + [
            pltpu.VMEM((TILE, TILE), low),
            pltpu.VMEM((TILE, D), low),
            pltpu.VMEM((2 * D, D), low),
            pltpu.VMEM((UNITS, UNIT, D), low),
            pltpu.VMEM((UNITS, UNIT, D), low),
            pltpu.VMEM((UNITS, 3, 64, D), low),
            pltpu.VMEM((UNITS, 64, D), f32),
            pltpu.VMEM((UNITS, 64, D), low),
            pltpu.VMEM((UNITS, 3, 16, D), low),
            pltpu.VMEM((UNITS, 4, 16, D), f32),
            pltpu.VMEM((UNITS, 16, WIDE), low),
        ]
        + [dma((4,))]
        + [dma((2, 2))] * 2
        + [dma((2,))] * 2
        + [dma((2, 6))] * 4
        + [dma((UNITS,))] * 3
        + [dma((UNITS, 3))] * 10
        + [dma((UNITS, 4))] * 2,
        compiler_params=pltpu.CompilerParams(collective_id=0, has_side_effects=True, vmem_limit_bytes=62 << 20),
        name="head_sums",
    )(scale, offset, img, txt, img_head, txt_head)


def shards(image_features, text_features, image_head, text_head, scale, offset):
    rows = head_sums(scale, offset, image_features, text_features, image_head, text_head)
    return decoded(rows[:D]), decoded(rows[D:])


def solution(mesh):
    in_specs = (P(("blk", "dp"), None), P(("blk", "dp"), None), P(), P(), P(), P())
    out_specs = (P(), P())
    return jax.shard_map(shards, mesh=mesh, in_specs=in_specs, out_specs=out_specs, check_vma=False)
```

time: 924 us -> 107 us (0.12)
  waiting for transfers between devices: 836 us -> 0 us
  Pallas kernels: 0 us -> 95.7 us
  matrix products: 48.7 us -> 0 us
  local copies, waits for them, and re-layouts: 17.1 us -> 0 us
  between operations: 15.2 us -> 1.94 us
    reduce_scatter x2 -> x0, waiting for transfers between devices: 460 us -> none  [the longest x1 239 us: shards(): lax.psum_scatter(text_pull(coef_own, image_emb, temper).astype(jnp.bfloat...]
    all_gather x2 -> x0, waiting for transfers between devices: 208 us -> none  [the longest x1 108 us: shards(): visiting = lax.all_gather(arriving, 'dp', axis=0, tiled=True)]
    psum x1 -> x0, waiting for transfers between devices: 164 us -> none  [shards(): image_grad, text_grad = lax.psum((image_term, text_term), ('blk', 'dp'))]
    pallas_call x0 -> x1, Pallas kernels: none -> 95.7 us  [head_sums(): pl.pallas_call(kernel, out_shape=jax.ShapeDtypeStruct((2 * D, WIDE), low)...]
    dot_general x10 -> x0, matrix products: 48.7 us -> none  [the longest x2 13.7 us: pair_coef(): jnp.einsum('id,jd->ij', image_emb, text_emb, preferred_element_type=jnp.f...]
    unnamed x18 -> x0, local copies, waits for them, and re-layouts: 17.1 us -> none
  transfers between devices with their start and end apart: 7 -> 0, of which waited for: 6 -> 0; matrix products, arithmetic and copies ran while one was open for 5% -> 0% of each run, Pallas kernels for 0% -> 0%
where the time goes in v1:
time: 107 us
  Pallas kernels  95.7 us (89%)
  other arithmetic  9.04 us (8%)
  between operations  1.94 us (2%)
    pallas_call x1, Pallas kernels, head_sums(): pl.pallas_call(kernel, out_shape=jax.ShapeDtypeStruct((2 * D, WIDE), low)...  95.7 us
    select_n x1, other arithmetic, decoded(): return jnp.where(code < 0, -size, size)  7.6 us

profile of v1, /device:TPU:1, one launch (start us, length us, event | category | flops | bytes accessed | tf_op | source)
XLA Modules:
  0.0 106.7 jit_solution(4080893350625595617)
XLA Ops:
  1.9 95.7 %head_sums.1 = bf16[2304,1280]{1,0:T(8,128)(2,1)} custom-call(f32[1]{0:T(128)S(6)} %copy.8.scale, f32[1]{0:T(128)S(6)} %copy.9.offset, bf16[128,1152]{1,0:T(8,128)(2,1)} %img.1, bf16[128,1152]{1,0:T(8,128)(2,1)} %txt.1, bf16[1152,1152]{1,0:T(8,128)(2,1)} %img_head.1, bf16[1152,1152]{1,0:T(8,128)(2,1)} %txt_head.1), custom_call_target="tpu_custom_call" | custom-call | tf_op jit(solution)/shard_map/head_sums/pallas_call | solution.py:476
  97.6 1.4 %multiply_reduce_fusion = (f32[1152]{0:T(1024)S(1)}, f32[1152]{0:T(1024)S(1)}) fusion(bf16[2304,1280]{1,0:T(8,128)(2,1)} %head_sums.1), kind=kLoop, calls=%fused_computation.14 | loop fusion | flops 4608 | bytes 13824 | tf_op jit(solution)/shard_map/div | solution.py:55
  99.1 7.6 %negate_select_fusion = (f32[1152,1152]{1,0:T(8,128)}, f32[1152,1152]{1,0:T(8,128)}) fusion(f32[1152]{0:T(1024)S(1)} %get-tuple-element.2, bf16[2304,1280]{1,0:T(8,128)(2,1)} %head_sums.1, f32[1152]{0:T(1024)S(1)} %get-tuple-element.3), kind=kLoop, calls=%fused_computation | loop fusion | flops 21233664 | bytes 15934464 | tf_op jit(solution)/shard_map/jit(_where)/select_n | solution.py:56
